TPU v7x, 512 devices: a whole 4x8x8 slice. The times are simulated.
512 devices in a mesh: slab: 128 (over y, z, core), grp: 4 (over x).
Axes of the slice: x: 4, y: 8, z: 8, core: 2. Of those that a mesh axis runs over, the one named last changes fastest.
Arguments:
- u_now: float32 [3, 2048, 32, 128], P(None, 'slab', 'grp'), may hold values from -6 to 6
- u_prev: float32 [3, 2048, 32, 128], P(None, 'slab', 'grp'), may hold values from -6 to 6
- force: float32 [3, 2048, 32, 128], P(None, 'slab', 'grp'), may hold values from -6 to 6
- stiffness: float32 [2048, 32, 128], P('slab', 'grp'), may hold values from 0.5 to 2
- broken: int32 [512, 8, 32], P('slab', 'grp'), may hold values 0 or 1
- flags: int32 [512, 8, 32], P('slab', 'grp'), may hold values 0 or 1
Outputs:
- displacement: float32 [3, 2048, 32, 128], P(None, 'slab', 'grp')
- coeffs: float32 [6, 32, 128, 2048], P(None, 'grp', 'slab')
All inputs are finite; a program needn't handle non-finite values. No bound on the sum of `broken` or of `flags` on one device may be relied on, other than what follows from the above.
Results may differ from a plain program's by a relative error of at most 0.0001.
Values sent between devices are 32-bit elements; how exact they have to be, the bound alone decides.
No kernel may reach another device: no remote copies, remote signals or barrier semaphores. Data moves between devices by JAX's collectives and lax.ppermute only.
A program may use at most 64 MiB of HBM per device.

v0:
```python
import jax
import jax.numpy as jnp
import numpy as np
from jax import lax
from jax.sharding import PartitionSpec as P

STEPS = 2
ITERS = 2
LEVELS = 3
SPRING_NORMAL = 1.0
SPRING_SHEAR = 0.4
MASS_TERM = 1.0
CRACK_CUT = 0.9


def with_halo(block, sides, width):
    for axis, dim in sides:
        count = lax.axis_size(axis)
        forward = [(i, i + 1) for i in range(count - 1)]
        backward = [(target, source) for source, target in forward]
        low = lax.ppermute(
            lax.slice_in_dim(block, block.shape[dim] - width, None, axis=dim), axis, forward
        )
        high = lax.ppermute(lax.slice_in_dim(block, 0, width, axis=dim), axis, backward)
        block = jnp.concatenate([low, block, high], axis=dim)
    return block


def cosine_table():
    freq = np.arange(4)[:, None]
    place = np.arange(4)[None, :]
    factor = np.where(freq == 0, 0.5, np.sqrt(0.5))
    return factor * np.cos(np.pi * (2 * place + 1) * freq / 8.0)


def block_table(count):
    return jnp.asarray(np.kron(np.eye(count // 4), cosine_table()), jnp.float32)


def spread(mask):
    values = mask.astype(jnp.float32)
    size_a, size_b, size_c = values.shape
    wide = jnp.broadcast_to(values[:, None, :, None, :, None], (size_a, 4, size_b, 4, size_c, 4))
    return wide.reshape(size_a * 4, size_b * 4, size_c * 4)


def sides(padded, axis_index):
    leading = padded.ndim - 3

    def cut(offset):
        index_list = [slice(None)] * leading + [slice(1, -1)] * 3
        length = padded.shape[leading + axis_index]
        index_list[leading + axis_index] = slice(1 + offset, length - 1 + offset)
        return padded[tuple(index_list)]

    return (cut(1), cut(-1))


def springs(field, weight, field_pad, weight_pad):
    result = MASS_TERM * field
    for axis_index in range(3):
        upper_v, lower_v = sides(field_pad, axis_index)
        upper_w, lower_w = sides(weight_pad, axis_index)
        k_upper = 0.5 * (weight + upper_w)
        k_lower = 0.5 * (weight + lower_w)
        change = k_upper * (field - upper_v) + k_lower * (field - lower_v)
        coupling = jnp.array(
            [SPRING_NORMAL if comp == axis_index else SPRING_SHEAR for comp in range(3)],
            jnp.float32,
        ).reshape(3, 1, 1, 1)
        result = result + coupling * change
    return result


def faces(field):
    padded = with_halo(field, (("slab", 1), ("grp", 2)), 1)
    return jnp.pad(padded, ((0, 0), (0, 0), (0, 0), (1, 1)))


def stresses(carry, field_pad):
    rows_out = []
    for axis_index in range(3):
        upper_v, lower_v = sides(field_pad, axis_index)
        rows_out.append(SPRING_NORMAL * carry * 0.5 * (upper_v[axis_index] - lower_v[axis_index]))
    return jnp.stack(rows_out)


def single_sum(value):
    return lax.psum(value, ("slab", "grp"))


def lift(signal):
    even = signal[..., 0::2]
    odd = signal[..., 1::2]
    detail = odd - 0.5 * (even + jnp.roll(even, -1, axis=-1))
    approx = even + 0.25 * (jnp.roll(detail, 1, axis=-1) + detail)
    return (approx, detail)


def wavelet(signal):
    pieces = []
    approx = signal
    for level_index in range(LEVELS):
        approx, detail = lift(approx)
        pieces.insert(0, detail)
    return jnp.concatenate([approx] + pieces, axis=-1)


def body(u_now, u_prev, force, stiffness, broken, flags):
    weight = stiffness * (1.0 - CRACK_CUT * spread(broken))
    carry = spread(flags) * weight
    weight_pad = with_halo(weight, (("slab", 0), ("grp", 1)), 1)
    weight_pad = jnp.pad(weight_pad, ((0, 0), (0, 0), (1, 1)))

    def operate(field):
        return springs(field, weight, faces(field), weight_pad)

    for step_index in range(STEPS):
        rhs = MASS_TERM * (2.0 * u_now - u_prev) + force
        guess = u_now
        residual = rhs - operate(guess)
        direction = residual
        norm_now = single_sum(jnp.sum(residual * residual))
        for turn_index in range(ITERS):
            image = operate(direction)
            alpha = norm_now / single_sum(jnp.sum(direction * image))
            guess = guess + alpha * direction
            residual = residual - alpha * image
            if turn_index + 1 < ITERS:
                norm_next = single_sum(jnp.sum(residual * residual))
                direction = residual + norm_next / norm_now * direction
                norm_now = norm_next
        u_prev = u_now
        u_now = guess
    stress = stresses(carry, faces(u_now))
    fields = jnp.concatenate([u_now, stress], axis=0)
    table_x = block_table(fields.shape[1])
    table_y = block_table(fields.shape[2])
    table_z = block_table(fields.shape[3])
    blockc = jnp.einsum("ax,hxyz->hayz", table_x, fields, precision=lax.Precision.HIGHEST)
    blockc = jnp.einsum("by,hxyz->hxbz", table_y, blockc, precision=lax.Precision.HIGHEST)
    blockc = jnp.einsum("hxyz,cz->hxyc", blockc, table_z, precision=lax.Precision.HIGHEST)
    moved = jnp.transpose(blockc, (0, 2, 3, 1))
    shipped = lax.all_to_all(moved, "slab", split_axis=2, concat_axis=3, tiled=True)
    coeffs = wavelet(shipped)
    return (u_now, coeffs)


def solution(mesh):
    return jax.shard_map(
        body,
        mesh=mesh,
        in_specs=(
            P(None, "slab", "grp", None),
            P(None, "slab", "grp", None),
            P(None, "slab", "grp", None),
            P("slab", "grp", None),
            P("slab", "grp", None),
            P("slab", "grp", None),
        ),
        out_specs=(P(None, "slab", "grp", None), P(None, "grp", "slab", None)),
        check_vma=False,
    )
```

profile of v0, /device:TPU:1, one launch (start us, length us, event | category | flops | bytes accessed | tf_op | source)
XLA Modules:
  0.0 816.2 jit_solution(5298064619461524530)
XLA Ops:
  3.5 5.4 collective-permute-start.2
  8.9 4.7 collective-permute-start
  15.5 3.6 collective-permute-start.3
  21.9 4.0 collective-permute-start.7
  31.6 3.8 collective-permute-start.9
  44.8 3.4 collective-permute-done.10
  49.5 106.3 %all-reduce.9 = (f32[]{:T(128)}, f32[]{:T(128)}) all-reduce(f32[]{:T(128)} %get-tuple-element.11, f32[]{:T(128)} %get-tuple-element.10), channel_id=1, replica_groups=mesh['slab'=128,'grp'=4] {'slab','grp'}, use_global_device_ids=true, to_apply=%region_1.2 | all-reduce | flops 2 | bytes 16 | tf_op jit(solution)/shard_map/psum | solution.py:89
  157.7 95.6 %psum.58 = f32[]{:T(128)} all-reduce(f32[]{:T(128)} %multiply_reduce_fusion.3), channel_id=1, replica_groups=mesh['slab'=128,'grp'=4] {'slab','grp'}, use_global_device_ids=true, to_apply=%region_5.6 | all-reduce | flops 1 | bytes 8 | tf_op jit(solution)/shard_map/psum | solution.py:89
  266.1 3.4 collective-permute-done.14
  270.7 100.4 %psum.59 = f32[]{:T(128)} all-reduce(f32[]{:T(128)} %fusion.75), channel_id=1, replica_groups=mesh['slab'=128,'grp'=4] {'slab','grp'}, use_global_device_ids=true, to_apply=%region_7.8 | all-reduce | flops 1 | bytes 8 | tf_op jit(solution)/shard_map/psum | solution.py:89
  379.6 3.7 collective-permute-start.19
  384.6 3.4 collective-permute-done.18
  388.6 3.6 collective-permute-start.21
  400.0 3.4 collective-permute-done.22
  404.7 105.3 %all-reduce.8 = (f32[]{:T(128)}, f32[]{:T(128)}) all-reduce(f32[]{:T(128)} %get-tuple-element.9, f32[]{:T(128)} %get-tuple-element.8), channel_id=1, replica_groups=mesh['slab'=128,'grp'=4] {'slab','grp'}, use_global_device_ids=true, to_apply=%region_9.10 | all-reduce | flops 2 | bytes 16 | tf_op jit(solution)/shard_map/psum | solution.py:89
  511.9 95.4 %psum.62 = f32[]{:T(128)} all-reduce(f32[]{:T(128)} %multiply_reduce_fusion), channel_id=1, replica_groups=mesh['slab'=128,'grp'=4] {'slab','grp'}, use_global_device_ids=true, to_apply=%region_13.14 | all-reduce | flops 1 | bytes 8 | tf_op jit(solution)/shard_map/psum | solution.py:89
  616.0 3.4 collective-permute-start.27
  625.4 100.4 %psum.63 = f32[]{:T(128)} all-reduce(f32[]{:T(128)} %fusion.15), channel_id=1, replica_groups=mesh['slab'=128,'grp'=4] {'slab','grp'}, use_global_device_ids=true, to_apply=%region_15.16 | all-reduce | flops 1 | bytes 8 | tf_op jit(solution)/shard_map/psum | solution.py:89
  734.2 3.7 collective-permute-start.31
  749.3 14.6 %all-to-all-start = ((f32[128,1,768]{2,1,0:T(1,128)}), f32[128,1,768]{2,1,0:T(1,128)S(1)}, u32[]{:S(2)}, u32[]{:S(2)}) async-start(f32[128,1,768]{2,1,0:T(1,128)} %reshape.66), calls=%async_computation | async-start | bytes 786432 | tf_op jit(solution)/shard_map/all_to_all | solution.py:144
  764.7 16.0 %all-to-all-done = f32[128,1,768]{2,1,0:T(1,128)S(1)} async-done(((f32[128,1,768]{2,1,0:T(1,128)}), f32[128,1,768]{2,1,0:T(1,128)S(1)}, u32[]{:S(2)}, u32[]{:S(2)}) %all-to-all-start) | async-done | bytes 393248 | tf_op jit(solution)/shard_map/all_to_all | solution.py:144
  786.4 3.8 all_to_all.10
  790.1 6.7 slice.508
  796.8 6.9 slice.509
  (150 shorter events, 105.6 us)
Async XLA Ops:
  3.5 15.7 %collective-permute-start.2 = (f32[1,8,128]{2,0,1:T(1,128)S(1)}, f32[1,8,128]{2,0,1:T(1,128)S(1)}, u32[]{:S(2)}, u32[]{:S(2)}) collective-permute-start(f32[1,8,128]{2,0,1:T(1,128)S(1)} %get-tuple-element.59), channel_id=1, source_target_pairs={{0,4},{4,8},{8,12},{12,16},{16,20},{20,24},{24,28},{28,32},{32,36}... | collective-permute-start | bytes 12296 | tf_op jit(solution)/shard_map/ppermute | solution.py:21
  8.9 10.4 %collective-permute-start = (f32[1,8,128]{2,0,1:T(1,128)S(1)}, f32[1,8,128]{2,0,1:T(1,128)S(1)}, u32[]{:S(2)}, u32[]{:S(2)}) collective-permute-start(f32[1,8,128]{2,0,1:T(1,128)S(1)} %get-tuple-element.60), channel_id=1, source_target_pairs={{4,0},{8,4},{12,8},{16,12},{20,16},{24,20},{28,24},{32,28},{36,32}... | collective-permute-start | bytes 12296 | tf_op jit(solution)/shard_map/ppermute | solution.py:24
  13.6 8.3 %collective-permute-start.1 = (f32[3,1,8,128]{3,1,2,0:T(1,128)S(1)}, f32[3,1,8,128]{3,1,2,0:T(1,128)S(1)}, u32[]{:S(2)}, u32[]{:S(2)}) collective-permute-start(f32[3,1,8,128]{3,1,2,0:T(1,128)S(1)} %bitcast.62), channel_id=1, source_target_pairs={{4,0},{8,4},{12,8},{16,12},{20,16},{24,20},{28,24},{32,28},{36,32}... | collective-permute-start | bytes 36872 | tf_op jit(solution)/shard_map/ppermute | solution.py:24
  15.5 6.3 collective-permute-start.3
  19.2 7.9 collective-permute-start.6
  20.5 6.7 collective-permute-start.4
  21.9 5.6 collective-permute-start.7
  25.9 5.0 collective-permute-start.5
  31.6 5.7 collective-permute-start.9
  35.4 5.0 collective-permute-start.8
  43.5 4.7 collective-permute-start.10
  257.0 5.0 collective-permute-start.12
  264.8 4.7 collective-permute-start.14
  374.5 5.0 collective-permute-start.16
  379.6 5.0 collective-permute-start.19
  388.6 5.5 collective-permute-start.21
  392.2 5.0 collective-permute-start.20
  398.7 4.7 collective-permute-start.22
  611.0 5.0 collective-permute-start.24
  616.0 4.7 collective-permute-start.27
  729.2 5.0 collective-permute-start.28
  734.2 7.0 collective-permute-start.31
  737.9 4.7 collective-permute-start.30
  749.3 31.3 %all-to-all-start = ((f32[128,1,768]{2,1,0:T(1,128)}), f32[128,1,768]{2,1,0:T(1,128)S(1)}, u32[]{:S(2)}, u32[]{:S(2)}) async-start(f32[128,1,768]{2,1,0:T(1,128)} %reshape.66), calls=%async_computation | async-start | bytes 786432 | tf_op jit(solution)/shard_map/all_to_all | solution.py:144
  (20 other events, 559.6 us)
where the time goes:
time: 826 us; the launch traced here: 816 us
  blocking collectives  603 us (73%)
  starting transfers between devices  92.5 us (11%)
  waiting for transfers between devices  54.8 us (7%)
  local copies, waits for them, and re-layouts  41.9 us (5%)
  other arithmetic  11.5 us (1%)
  between operations  9.84 us (1%)
    psum x6, blocking collectives, single_sum(): return lax.psum(value, ('slab', 'grp'))  603 us
    ppermute x16, starting transfers between devices, with_halo(): lax.ppermute(lax.slice_in_dim(block, block.shape[dim] - width, None, axis...  48 us
    ppermute x16, waiting for transfers between devices, with_halo(): lax.ppermute(lax.slice_in_dim(block, 0, width, axis=dim), axis, backward)  38.8 us
    ppermute x16, starting transfers between devices, with_halo(): lax.ppermute(lax.slice_in_dim(block, 0, width, axis=dim), axis, backward)  29.8 us
  transfers between devices with their start and end apart: 33, of which 14 were waited for; matrix products, arithmetic and copies ran while one was open for 0% of the time, Pallas kernels for 0%

commit v1 on v0

--- a/solution.py
+++ b/solution.py
@@ -86,7 +86,7 @@
 
 
 def single_sum(value):
-    return lax.psum(value, ("slab", "grp"))
+    return lax.psum(lax.psum(value, "grp"), "slab")
 
 
 def lift(signal):

time: 826 us -> 1790 us (2.17)
  blocking collectives: 603 us -> 1540 us
  starting transfers between devices: 92.5 us -> 123 us
    psum x6 -> x12, blocking collectives: 603 us -> 1540 us  [single_sum(): return lax.psum(lax.psum(value, 'grp'), 'slab')]
    all_to_all x1, starting transfers between devices: 14.6 us -> 45.6 us  [body(): lax.all_to_all(moved, 'slab', split_axis=2, concat_axis=3, tiled=True)]
where the time goes in v1:
time: 1790 us; the launch traced here: 1780 us
  blocking collectives  1540 us (86%)
  starting transfers between devices  123 us (7%)
  waiting for transfers between devices  53.8 us (3%)
  local copies, waits for them, and re-layouts  41.9 us (2%)
    psum x12, blocking collectives, single_sum(): return lax.psum(lax.psum(value, 'grp'), 'slab')  1540 us
    ppermute x16, starting transfers between devices, with_halo(): lax.ppermute(lax.slice_in_dim(block, block.shape[dim] - width, None, axis...  47 us
    all_to_all x1, starting transfers between devices, body(): lax.all_to_all(moved, 'slab', split_axis=2, concat_axis=3, tiled=True)  45.6 us
    ppermute x16, waiting for transfers between devices, with_halo(): lax.ppermute(lax.slice_in_dim(block, 0, width, axis=dim), axis, backward)  37.8 us
  transfers between devices with their start and end apart: 33, of which 14 were waited for; matrix products, arithmetic and copies ran while one was open for 0% of the time, Pallas kernels for 0%

profile of v1, /device:TPU:1, one launch (start us, length us, event | category | flops | bytes accessed | tf_op | source)
XLA Modules:
  0.0 1783.6 jit_solution(1184914103566601014)
XLA Ops:
  3.5 5.4 collective-permute-start.2
  8.9 4.7 collective-permute-start
  15.5 3.6 collective-permute-start.3
  21.9 4.0 collective-permute-start.7
  31.6 3.8 collective-permute-start.9
  49.5 7.8 all-reduce.11
  57.3 254.5 %all-reduce.9 = (f32[]{:T(128)}, f32[]{:T(128)}) all-reduce(f32[]{:T(128)} %get-tuple-element.18, f32[]{:T(128)} %get-tuple-element.19), channel_id=1, replica_groups=mesh['slab'=128,'grp'=4] {'slab'}, use_global_device_ids=true, to_apply=%region_2.3 | all-reduce | flops 2 | bytes 16 | tf_op jit(solution)/shard_map/psum | solution.py:89
  313.7 7.1 psum.116
  320.8 249.0 %psum.117 = f32[]{:T(128)} all-reduce(f32[]{:T(128)} %psum.116), channel_id=1, replica_groups=mesh['slab'=128,'grp'=4] {'slab'}, use_global_device_ids=true, to_apply=%region_8.9 | all-reduce | flops 1 | bytes 8 | tf_op jit(solution)/shard_map/psum | solution.py:89
  586.9 6.6 psum.118
  593.6 248.5 %psum.119 = f32[]{:T(128)} all-reduce(f32[]{:T(128)} %psum.118), channel_id=1, replica_groups=mesh['slab'=128,'grp'=4] {'slab'}, use_global_device_ids=true, to_apply=%region_11.12 | all-reduce | flops 1 | bytes 8 | tf_op jit(solution)/shard_map/psum | solution.py:89
  850.5 3.6 collective-permute-start.19
  875.5 8.0 all-reduce.10
  883.5 248.0 %all-reduce.8 = (f32[]{:T(128)}, f32[]{:T(128)}) all-reduce(f32[]{:T(128)} %get-tuple-element.16, f32[]{:T(128)} %get-tuple-element.17), channel_id=1, replica_groups=mesh['slab'=128,'grp'=4] {'slab'}, use_global_device_ids=true, to_apply=%region_14.15 | all-reduce | flops 2 | bytes 16 | tf_op jit(solution)/shard_map/psum | solution.py:89
  1133.5 7.0 psum.124
  1140.5 249.4 %psum.125 = f32[]{:T(128)} all-reduce(f32[]{:T(128)} %psum.124), channel_id=1, replica_groups=mesh['slab'=128,'grp'=4] {'slab'}, use_global_device_ids=true, to_apply=%region_20.21 | all-reduce | flops 1 | bytes 8 | tf_op jit(solution)/shard_map/psum | solution.py:89
  1407.3 6.6 psum.126
  1413.9 248.5 %psum.127 = f32[]{:T(128)} all-reduce(f32[]{:T(128)} %psum.126), channel_id=1, replica_groups=mesh['slab'=128,'grp'=4] {'slab'}, use_global_device_ids=true, to_apply=%region_23.24 | all-reduce | flops 1 | bytes 8 | tf_op jit(solution)/shard_map/psum | solution.py:89
  1670.8 3.6 collective-permute-start.31
  1685.8 45.6 %all-to-all-start = ((f32[128,1,768]{2,1,0:T(1,128)}), f32[128,1,768]{2,1,0:T(1,128)S(1)}, u32[]{:S(2)}, u32[]{:S(2)}) async-start(f32[128,1,768]{2,1,0:T(1,128)} %reshape.66), calls=%async_computation | async-start | bytes 786432 | tf_op jit(solution)/shard_map/all_to_all | solution.py:144
  1732.1 16.0 all-to-all-done
  1753.8 3.8 all_to_all.10
  1757.6 6.7 slice.508
  1764.2 6.9 slice.509
  (156 shorter events, 125.3 us)
Async XLA Ops:
  3.5 15.7 collective-permute-start.2
  8.9 10.4 collective-permute-start
  13.6 8.3 collective-permute-start.1
  15.5 6.3 collective-permute-start.3
  19.2 7.9 collective-permute-start.6
  20.5 6.7 collective-permute-start.4
  21.9 5.6 collective-permute-start.7
  25.9 5.0 collective-permute-start.5
  31.6 5.7 collective-permute-start.9
  35.4 5.0 collective-permute-start.8
  43.5 4.7 collective-permute-start.10
  573.1 5.0 collective-permute-start.12
  581.0 4.7 collective-permute-start.14
  845.4 5.0 collective-permute-start.16
  850.5 4.9 collective-permute-start.19
  854.1 4.7 collective-permute-start.18
  859.5 5.3 collective-permute-start.21
  862.9 5.0 collective-permute-start.20
  1393.2 5.0 collective-permute-start.24
  1401.3 4.7 collective-permute-start.26
  1665.7 5.0 collective-permute-start.28
  1670.8 7.4 collective-permute-start.31
  1674.4 4.7 collective-permute-start.30
  1685.8 62.3 %all-to-all-start = ((f32[128,1,768]{2,1,0:T(1,128)}), f32[128,1,768]{2,1,0:T(1,128)S(1)}, u32[]{:S(2)}, u32[]{:S(2)}) async-start(f32[128,1,768]{2,1,0:T(1,128)} %reshape.66), calls=%async_computation | async-start | bytes 786432 | tf_op jit(solution)/shard_map/all_to_all | solution.py:144
  (20 other events, 1024.6 us)
